TPU v7x, 128 devices: a whole 4x4x4 slice. The times are simulated.
128 devices in a mesh: blk: 32 (over x, y, z_hi), head: 4 (over z_lo, core).
Axes of the slice: x: 4, y: 4, z: 4 (z_hi: 2, z_lo: 2; z = z_hi * 2 + z_lo), core: 2. Of those that a mesh axis runs over, the one named last changes fastest.
Arguments:
- x_video: bfloat16 [16384, 3072], P(('blk', 'head')), may hold values from -6 to 6
- x_text: bfloat16 [256, 3072], replicated, may hold values from -6 to 6
- w_qkv_video: bfloat16 [3072, 3, 1536], P(None, None, 'head'), may hold values from -0.109375 to 0.109375
- w_qkv_text: bfloat16 [3072, 3, 1536], P(None, None, 'head'), may hold values from -0.109375 to 0.109375
- w_out_video: bfloat16 [1536, 3072], P('head'), may hold values from -0.15625 to 0.15625
- w_out_text: bfloat16 [1536, 3072], P('head'), may hold values from -0.15625 to 0.15625
- qk_gains: float32 [4, 128], replicated, may hold values from 0.8 to 1.4
- modulation: float32 [50, 6, 3072], replicated, may hold values from -3 to 3
- text_len: int32 [1], replicated, may hold values from 64 to 256
- timestep: int32 [1], replicated, may hold values from 0 to 49
Outputs:
- video_out: bfloat16 [16384, 3072], P(('blk', 'head'))
- text_out: bfloat16 [256, 3072], P('head')
All inputs are finite; a program needn't handle non-finite values.
Results may differ from a plain program's by a relative error of at most 0.0052.
Values may be sent and summed in bfloat16 or wider, within the bound.
A program may use at most 192 MiB of HBM per device.

v0:
```python
import math

import jax
import jax.numpy as jnp
from jax import lax
from jax.sharding import PartitionSpec as P

HEAD_DIM = 128


def norm_modulate(tokens, shift, scale):
    wide = tokens.astype(jnp.float32)
    centred = wide - jnp.mean(wide, axis=-1, keepdims=True)
    variance = jnp.mean(centred * centred, axis=-1, keepdims=True)
    return (centred * lax.rsqrt(variance + 1e-06) * (1.0 + scale) + shift).astype(jnp.bfloat16)


def head_norm(values, gain):
    count, width = values.shape
    split = values.reshape(count, width // HEAD_DIM, HEAD_DIM)
    meansq = jnp.mean(split * split, axis=-1, keepdims=True)
    return (split * lax.rsqrt(meansq + 1e-06) * gain).reshape(count, width).astype(jnp.bfloat16)


def project_stack(normed, weight, gain_query, gain_key):
    width = weight.shape[2]
    flat = jnp.dot(
        normed, weight.reshape(weight.shape[0], 3 * width), preferred_element_type=jnp.float32
    )
    queries = head_norm(flat[:, :width], gain_query)
    key_rows = head_norm(flat[:, width : 2 * width], gain_key)
    value_rows = flat[:, 2 * width :].astype(jnp.bfloat16)
    return jnp.stack([queries, key_rows, value_rows], axis=1)


def partial_scores(queries, key_rows, value_rows, key_mask):
    count, width = queries.shape
    nheads = width // HEAD_DIM
    query_split = queries.reshape(count, nheads, HEAD_DIM)
    key_split = key_rows.reshape(-1, nheads, HEAD_DIM)
    value_split = value_rows.reshape(-1, nheads, HEAD_DIM)
    scores = jnp.einsum(
        "qhd,khd->hqk", query_split, key_split, preferred_element_type=jnp.float32
    ) * HEAD_DIM ** (-0.5)
    expo = jnp.exp(scores)
    if key_mask is not None:
        expo = expo * key_mask[None, None, :]
    weights = expo.astype(jnp.bfloat16)
    numer = jnp.einsum(
        "hqk,khd->qhd", weights, value_split, preferred_element_type=jnp.float32
    ).reshape(count, width)
    denom = jnp.sum(expo, axis=2).T
    return (numer, denom)


def add_keys(running, queries, key_rows, value_rows):
    count = key_rows.shape[0]
    block_size = math.gcd(count, 512)
    nblocks = count // block_size
    key_blocks = key_rows.reshape(nblocks, block_size, key_rows.shape[1])
    value_blocks = value_rows.reshape(nblocks, block_size, value_rows.shape[1])

    def advance(totals, key_pair):
        numer, denom = partial_scores(queries, key_pair[0], key_pair[1], None)
        return ((totals[0] + numer, totals[1] + denom), None)

    result, unused = lax.scan(advance, running, (key_blocks, value_blocks))
    return result


def finish(numer, denom):
    count, width = numer.shape
    split = numer.reshape(count, denom.shape[1], HEAD_DIM) / denom[:, :, None]
    return split.reshape(count, width).astype(jnp.bfloat16)


def body(
    x_video,
    x_text,
    w_qkv_video,
    w_qkv_text,
    w_out_video,
    w_out_text,
    qk_gains,
    modulation,
    text_len,
    timestep,
):
    step_count = modulation.shape[0]
    picked = lax.broadcasted_iota(jnp.int32, (step_count, 1, 1), 0) == timestep[0]
    mods = jnp.sum(jnp.where(picked, modulation, 0.0), axis=0)
    normed_video = norm_modulate(x_video, mods[0], mods[1])
    normed_text = norm_modulate(x_text, mods[3], mods[4])
    video_stack = project_stack(
        lax.all_gather(normed_video, "head", axis=0, tiled=True),
        w_qkv_video,
        qk_gains[0],
        qk_gains[1],
    )
    q_video, k_video, v_video = (video_stack[:, 0], video_stack[:, 1], video_stack[:, 2])
    text_stack = project_stack(normed_text, w_qkv_text, qk_gains[2], qk_gains[3])
    q_text, k_text, v_text = (text_stack[:, 0], text_stack[:, 1], text_stack[:, 2])
    text_total = x_text.shape[0]
    text_valid = jnp.arange(text_total, dtype=jnp.int32) < text_len[0]
    text_mask = text_valid.astype(jnp.float32)
    video_init = partial_scores(q_video, k_text, v_text, text_mask)
    video_numer, video_denom = add_keys(
        video_init,
        q_video,
        lax.all_gather(k_video, "blk", axis=0, tiled=True),
        lax.all_gather(v_video, "blk", axis=0, tiled=True),
    )
    local_numer, local_denom = partial_scores(q_text, k_video, v_video, None)
    summed_numer, summed_denom = lax.psum((local_numer, local_denom), "blk")
    own_numer, own_denom = partial_scores(q_text, k_text, v_text, text_mask)
    attn_text = finish(summed_numer + own_numer, summed_denom + own_denom)
    attn_video = finish(video_numer, video_denom)
    block = attn_video
    video_summed = lax.psum_scatter(
        jnp.dot(block, w_out_video, preferred_element_type=jnp.float32),
        "head",
        scatter_dimension=0,
        tiled=True,
    )
    video_out = (mods[2] * video_summed).astype(jnp.bfloat16)
    head_count = lax.axis_size("head")
    text_share = text_total // head_count
    block = attn_text
    text_summed = lax.psum_scatter(
        jnp.dot(block, w_out_text, preferred_element_type=jnp.float32),
        "head",
        scatter_dimension=0,
        tiled=True,
    )
    row_index = lax.axis_index("head") * text_share + jnp.arange(text_share, dtype=jnp.int32)
    text_out = jnp.where((row_index < text_len[0])[:, None], mods[5] * text_summed, 0.0).astype(
        jnp.bfloat16
    )
    return (video_out, text_out)


def solution(mesh):
    return jax.shard_map(
        body,
        mesh=mesh,
        in_specs=(
            P(("blk", "head"), None),
            P(),
            P(None, None, "head"),
            P(None, None, "head"),
            P("head", None),
            P("head", None),
            P(),
            P(),
            P(),
            P(),
        ),
        out_specs=(P(("blk", "head"), None), P("head", None)),
        check_vma=False,
    )
```

profile of v0, /device:TPU:1, one launch (start us, length us, event | category | flops | bytes accessed | tf_op | source)
XLA Modules:
  0.0 1064.3 jit_solution(13134364867765886232)
XLA Ops:
  8.1 2.9 select_reduce_fusion
  13.5 10.3 copy.29
  26.3 5.9 fusion.15
  48.9 10.3 copy.31
  59.2 8.2 fusion.36
  75.0 2.8 multiply_convert_fusion.1
  88.5 85.1 %psum.15 = f32[256,3]{0,1:T(4,128)S(1)} all-reduce(f32[256,3]{0,1:T(4,128)S(1)} %bitcast.157), channel_id=1, replica_groups=mesh['blk'=32,'head'=4] {'blk'}, use_global_device_ids=true, to_apply=%region_16.17 | all-reduce | flops 768 | bytes 6144 | tf_op jit(solution)/shard_map/psum | solution.py:114
  176.2 227.9 %all-reduce.2.cloned.1.call-done = f32[256,384]{0,1:T(8,128)} async-done(((f32[256,384]{0,1:T(8,128)}), f32[256,384]{0,1:T(8,128)}) %all-reduce.2.cloned.1.call-update) | async-done | bytes 393232 | tf_op jit(solution)/shard_map/psum | solution.py:114
  405.1 4.4 fusion.38
  409.6 142.8 %all-gather.8.cloned.1.call-done = bf16[16384,384]{1,0:T(8,128)(2,1)} async-done(((bf16[512,384]{1,0:T(8,128)(2,1)}), bf16[16384,384]{1,0:T(8,128)(2,1)}) %all-gather.8.cloned.1.call-update) | async-done | bytes 12582928 | tf_op jit(solution)/shard_map/all_gather | solution.py:110
  552.4 131.0 %all-gather.6.cloned.1.call-done = bf16[16384,384]{1,0:T(8,128)(2,1)} async-done(((bf16[512,384]{1,0:T(8,128)(2,1)}), bf16[16384,384]{1,0:T(8,128)(2,1)}) %all-gather.6.cloned.1.call-update) | async-done | bytes 12582928 | tf_op jit(solution)/shard_map/all_gather | solution.py:111
  683.4 304.6 %while.12 = (s32[]{:T(128)}, f32[512,384]{0,1:T(8,128)}, f32[512,3]{0,1:T(4,128)S(1)}, bf16[32,512,384]{2,1,0:T(8,128)(2,1)}, bf16[32,512,384]{2,1,0:T(8,128)(2,1)}, /*index=5*/bf16[512,384]{0,1:T(8,128)(2,1)S(1)}, s32[]{:T(128)}) while((s32[]{:T(128)}, f32[512,384]{0,1:T(8,128)}, f32[512,3]{0,1:T(4,128)S(1)}, ...), condition=%wide.region_11.12_spmd, body=%wide.region_9.0_spmd.sunk | while | flops 405995520 | bytes 23224512 | solution.py:67
  685.6 3.4 bitcast_reduce_fusion.2
  695.1 3.4 bitcast_reduce_fusion.2
  704.6 3.4 bitcast_reduce_fusion.2
  708.2 2.7 fusion.68
  714.2 3.4 bitcast_reduce_fusion.2
  717.8 2.7 fusion.68
  723.7 3.4 bitcast_reduce_fusion.2
  733.2 3.4 bitcast_reduce_fusion.2
  742.8 3.4 bitcast_reduce_fusion.2
  752.3 3.4 bitcast_reduce_fusion.2
  761.8 3.4 bitcast_reduce_fusion.2
  771.3 3.4 bitcast_reduce_fusion.2
  780.8 3.4 bitcast_reduce_fusion.2
  790.3 3.4 bitcast_reduce_fusion.2
  799.8 3.4 bitcast_reduce_fusion.2
  809.4 3.4 bitcast_reduce_fusion.2
  818.9 3.4 bitcast_reduce_fusion.2
  828.4 3.4 bitcast_reduce_fusion.2
  837.9 3.4 bitcast_reduce_fusion.2
  847.4 3.4 bitcast_reduce_fusion.2
  856.9 3.4 bitcast_reduce_fusion.2
  866.5 3.4 bitcast_reduce_fusion.2
  876.0 3.4 bitcast_reduce_fusion.2
  885.5 3.4 bitcast_reduce_fusion.2
  895.0 3.4 bitcast_reduce_fusion.2
  904.5 3.4 bitcast_reduce_fusion.2
  914.0 3.4 bitcast_reduce_fusion.2
  923.6 3.4 bitcast_reduce_fusion.2
  933.1 3.4 bitcast_reduce_fusion.2
  942.6 3.4 bitcast_reduce_fusion.2
  952.1 3.4 bitcast_reduce_fusion.2
  961.6 3.4 bitcast_reduce_fusion.2
  971.1 3.4 bitcast_reduce_fusion.2
  980.6 3.4 bitcast_reduce_fusion.2
  989.2 4.5 fusion.37
  996.4 58.6 %reduce-scatter.3.cloned.1.call-done = f32[128,3072]{1,0:T(8,128)} async-done(((f32[512,3072]{1,0:T(8,128)}), f32[128,3072]{1,0:T(8,128)}) %reduce-scatter.3.cloned.1.call-update) | async-done | bytes 1572880 | tf_op jit(solution)/shard_map/reduce_scatter | solution.py:119
  (548 shorter events, 236.9 us)
Async XLA Ops:
  7.2 982.1 %copy-start = (bf16[384,3072]{1,0:T(8,128)(2,1)S(1)}, bf16[384,3072]{1,0:T(8,128)(2,1)}, u32[]{:S(2)}) copy-start(bf16[384,3072]{1,0:T(8,128)(2,1)} %param.16) | copy-start | bytes 7077892
  7.2 4.4 copy-start.5
  7.2 52.0 %all-gather.4.cloned.1.call-start = ((), (), s32[]{:S(2)}) async-start(), calls=%async_computation.2 | async-start | bytes 3932160 | tf_op jit(solution)/shard_map/all_gather | solution.py:95
  13.5 390.6 %all-reduce.2.cloned.1.call-start = ((), (), s32[]{:S(2)}) async-start(), calls=%async_computation.6 | async-start | bytes 786432 | tf_op jit(solution)/shard_map/psum | solution.py:114
  32.2 12.9 %copy-start.10 = (f32[256,1152]{1,0:T(8,128)}, f32[256,1152]{1,0:T(8,128)S(1)}, u32[]{:S(2)}) copy-start(f32[256,1152]{1,0:T(8,128)S(1)} %fusion.15) | copy-start | bytes 3538948
  33.2 11.3 %copy-start.17 = (f32[4,128]{1,0:T(4,128)S(1)}, f32[4,128]{1,0:T(4,128)}, u32[]{:S(2)}) copy-start(f32[4,128]{1,0:T(4,128)} %param.18) | copy-start | bytes 6148
  48.9 10.3 copy-start.18
  69.3 9.4 copy-start.9
  77.8 3.9 copy-start.8
  81.7 6.6 copy-start.11
  81.7 470.7 %all-gather.8.cloned.1.call-start = ((), (), s32[]{:S(2)}) async-start(), calls=%async_computation.4 | async-start | bytes 12976128 | tf_op jit(solution)/shard_map/all_gather | solution.py:110
  82.4 601.0 %all-gather.6.cloned.1.call-start = ((), (), s32[]{:S(2)}) async-start(), calls=%async_computation.3 | async-start | bytes 12976128 | tf_op jit(solution)/shard_map/all_gather | solution.py:111
  83.0 910.8 %reduce-scatter.5.cloned.1.call-start = ((), (), s32[]{:S(2)}) async-start(), calls=%async_computation.7 | async-start | bytes 3932160 | tf_op jit(solution)/shard_map/reduce_scatter | solution.py:129
  88.5 315.6 %copy-start.12 = (f32[3,128,256]{2,1,0:T(8,128)S(1)}, f32[3,128,256]{2,1,0:T(8,128)}, u32[]{:S(2)}) copy-start(f32[3,128,256]{2,1,0:T(8,128)} %fusion.30) | copy-start | bytes 1179652
  409.6 645.5 %reduce-scatter.3.cloned.1.call-start = ((), (), s32[]{:S(2)}) async-start(), calls=%async_computation.5 | async-start | bytes 7864320 | tf_op jit(solution)/shard_map/reduce_scatter | solution.py:119
  689.2 3.8 copy-start.4
  698.7 3.8 copy-start.4
  708.2 3.8 copy-start.4
  717.8 3.8 copy-start.4
  727.3 3.7 copy-start.4
  736.9 3.8 copy-start.4
  746.4 3.8 copy-start.4
  755.9 3.8 copy-start.4
  765.4 3.8 copy-start.4
  774.9 3.8 copy-start.4
  784.4 3.8 copy-start.4
  793.9 3.8 copy-start.4
  803.5 3.8 copy-start.4
  813.0 3.8 copy-start.4
  822.5 3.8 copy-start.4
  832.0 3.8 copy-start.4
  841.5 3.8 copy-start.4
  851.0 3.8 copy-start.4
  860.6 3.8 copy-start.4
  870.1 3.8 copy-start.4
  879.6 3.8 copy-start.4
  889.1 3.8 copy-start.4
  898.6 3.8 copy-start.4
  908.1 3.8 copy-start.4
  917.7 3.8 copy-start.4
  927.2 3.8 copy-start.4
  936.7 3.8 copy-start.4
  946.2 3.8 copy-start.4
  955.7 3.8 copy-start.4
  965.2 3.8 copy-start.4
  974.7 3.8 copy-start.4
  984.3 3.8 copy-start.4
  993.7 61.3 %copy-start.14 = (f32[1,3072]{1,0:T(1,128)S(1)}, f32[1,3072]{1,0:T(1,128)}, u32[]{:S(2)}) copy-start(f32[1,3072]{1,0:T(1,128)} %get-tuple-element.78) | copy-start | bytes 36868
  (101 other events, 147.5 us)
Sparse Core Ops, SparseCore 0:
  13.6 41.5 all-gather.3
  81.8 322.1 all-reduce.1
  407.4 144.9 all-gather.7
  555.7 127.7 all-gather.5
  685.8 35.1 reduce-scatter.4
  993.9 61.0 reduce-scatter.2
where the time goes:
time: 1070 us; the launch traced here: 1060 us
  waiting for transfers between devices  562 us (53%)
  matrix products  224 us (21%)
  local copies, waits for them, and re-layouts  145 us (14%)
  blocking collectives  85.1 us (8%)
  other arithmetic  30.3 us (3%)
  between operations  15.8 us (1%)
    psum x1, waiting for transfers between devices, body(): summed_numer, summed_denom = lax.psum((local_numer, local_denom), 'blk')  228 us
    all_gather x1, waiting for transfers between devices, body(): lax.all_gather(k_video, 'blk', axis=0, tiled=True)  143 us
    all_gather x1, waiting for transfers between devices, body(): lax.all_gather(v_video, 'blk', axis=0, tiled=True)  131 us
    dot_general x35, matrix products, partial_scores(): jnp.einsum('qhd,khd->hqk', query_split, key_split, preferred_element_type...  113 us
    dot_general x35, matrix products, partial_scores(): jnp.einsum('hqk,khd->qhd', weights, value_split, preferred_element_type=j...  87.4 us
    psum x1, blocking collectives, body(): summed_numer, summed_denom = lax.psum((local_numer, local_denom), 'blk')  85.1 us
    reduce_scatter x1, waiting for transfers between devices, body(): lax.psum_scatter(jnp.dot(block, w_out_video, preferred_element_type=jnp.f...  58.6 us
    while x256, local copies, waits for them, and re-layouts  52.1 us
  transfers between devices with their start and end apart: 6, of which 4 were waited for; matrix products, arithmetic and copies ran while one was open for 30% of the time, Pallas kernels for 0%

commit v1 on v0

v1 whole, which is shorter than its diff:
```python
import functools
import math

import jax
import jax.numpy as jnp
from jax import lax
from jax.experimental import pallas as pl
from jax.experimental.pallas import tpu as pltpu
from jax.sharding import Mesh, PartitionSpec as P

AXES = ("x", "y", "zh", "zl", "c")
MESH = pl.DeviceIdType.MESH
BF16, F32 = jnp.bfloat16, jnp.float32
D = 3072
HD = 128
NH = 3
W = NH * HD
BLK = 512
TXT = 256
TQ = 32
OWN = BLK + TQ
QROWS = 4 * BLK + TQ
EXP_SCALE = math.log2(math.e) / math.sqrt(HD)
VMEM_LIMIT = 60 << 20


def coords():
    x, y, zh, zl, c = (lax.axis_index(a) for a in AXES)
    return x, y, zh * 2 + zl, c


def dev(x, y, z, c):
    z = lax.rem(z + 4, 4)
    return (lax.rem(x + 4, 4), lax.rem(y + 4, 4), z // 2, lax.rem(z, 2), c)


class Sends:
    def __init__(self, sems, peer):
        self.sems, self.peer, self.count, self.pending = sems, peer, 0, []

    def start(self, src, dst, recv_sem, device, pred=None):
        slot = self.count
        self.count += 1
        get = src if callable(src) else (lambda: src)

        pltpu.make_async_remote_copy(
            src_ref=get(), dst_ref=dst, send_sem=self.sems.at[slot], recv_sem=recv_sem,
            device_id=device, device_id_type=MESH).start()

        def wait():
            pltpu.make_async_remote_copy(
                src_ref=get(), dst_ref=get(), send_sem=self.sems.at[slot], recv_sem=self.sems.at[slot],
                device_id=self.peer, device_id_type=MESH).wait_send()

        self.pending.append((pred, wait))

    def finish(self):
        for pred, wait in self.pending:
            if pred is None:
                wait()
            else:
                pl.when(pred)(wait)


def signal(sem, device):
    pl.semaphore_signal(sem, inc=1, device_id=device, device_id_type=MESH)


def norm_rows(src, dst, dst_row, count, shift, scale1):
    def strip(i, carry):
        wide = src[pl.ds(pl.multiple_of(i * 16, 16), 16), :].astype(F32)
        centred = wide - jnp.mean(wide, axis=-1, keepdims=True)
        variance = jnp.mean(centred * centred, axis=-1, keepdims=True)
        out = centred * lax.rsqrt(variance + 1e-06) * scale1 + shift
        dst[pl.ds(pl.multiple_of(dst_row + i * 16, 16), 16), :] = out.astype(BF16)
        return carry

    lax.fori_loop(0, count // 16, strip, 0, unroll=2)


def project(rows, weight, out, out_row, gain_query, gain_key):
    flat = jnp.dot(rows, weight[...], preferred_element_type=F32)
    count = rows.shape[0]
    for part in range(3):
        for h in range(NH):
            u = flat[:, part * W + h * HD : part * W + (h + 1) * HD]
            if part < 2:
                gain = gain_query if part == 0 else gain_key
                meansq = jnp.mean(u * u, axis=-1, keepdims=True)
                u = u * lax.rsqrt(meansq + 1e-06) * gain
            out[part, out_row : out_row + count, h * HD : (h + 1) * HD] = u.astype(BF16)


def qkv_kernel(x_ref, xt_ref, wv_ref, wt_ref, mod_ref, gains_ref, wov_ref, wot_ref, step_ref,
               qkv_ref, tqkv_ref, wsv_ref, wst_ref,
               xb, xtb, wvb, wtb, modb, nb, load_sem, send_sem, x_sem, w_sem):
    x, y, z, c = coords()
    zh = z // 2
    role = lax.rem(c + zh, 2)
    sibling = dev(x, y, z, 1 - c)
    toward = z + 2 * c - 1
    loads = [
        pltpu.make_async_copy(x_ref, xb.at[c], load_sem.at[0]),
        pltpu.make_async_copy(mod_ref, modb, load_sem.at[1]),
        pltpu.make_async_copy(xt_ref, xtb, load_sem.at[2]),
    ]
    for part in range(3):
        loads.append(pltpu.make_async_copy(
            wt_ref.at[part], wtb.at[:, part * W : (part + 1) * W], load_sem.at[3 + part]))
    for part in range(3):
        loads.append(pltpu.make_async_copy(
            wv_ref.at[part], wvb.at[:, part * W : (part + 1) * W], load_sem.at[6 + part]))
    for copy in loads:
        copy.start()

    barrier = pltpu.get_barrier_semaphore()
    signal(barrier, sibling)
    signal(barrier, dev(x, y, z + 1, 0))
    signal(barrier, dev(x, y, z - 1, 1))
    pl.semaphore_wait(barrier, 3)

    sends = Sends(send_sem, sibling)
    for half in range(2):
        rows = pl.ds(half * 64, 64)
        sends.start(x_ref.at[rows], xb.at[2 + c, rows], x_sem.at[1 + c], dev(x, y, toward, half))
    sends.start(x_ref, xb.at[c], x_sem.at[0], sibling)
    sends.start(wov_ref, wsv_ref, w_sem.at[0], sibling)
    sends.start(wot_ref, wst_ref, w_sem.at[1], sibling)

    def arrived(dst, sem):
        pltpu.make_async_remote_copy(
            src_ref=dst, dst_ref=dst, send_sem=send_sem.at[0], recv_sem=sem,
            device_id=sibling, device_id_type=MESH).wait_recv()

    step = step_ref[0]
    loads[1].wait()
    loads[2].wait()
    for part in range(3):
        loads[3 + part].wait()

    @pl.when(role == 0)
    def _():
        norm_rows(xtb, nb, 0, TXT, modb[3, pl.ds(step, 1), :], 1.0 + modb[4, pl.ds(step, 1), :])
        project(nb[0:TXT, :], wtb, tqkv_ref, 0, gains_ref[2:3, :], gains_ref[3:4, :])

    shift, scale1 = modb[0, pl.ds(step, 1), :], 1.0 + modb[1, pl.ds(step, 1), :]
    loads[0].wait()
    arrived(xb.at[1 - c], x_sem.at[0])
    norm_rows(xb.at[0], nb, 0, 128, shift, scale1)
    norm_rows(xb.at[1], nb, 128, 128, shift, scale1)
    for part in range(3):
        loads[6 + part].wait()
    project(nb[0:256, :], wvb, qkv_ref, 0, gains_ref[0:1, :], gains_ref[1:2, :])

    mine = pl.ds(pl.multiple_of(c * 64, 64), 64)
    other = pl.ds(pl.multiple_of((1 - c) * 64, 64), 64)
    for slot in (2, 3):
        arrived(xb.at[slot, mine], x_sem.at[slot - 1])
        sends.start(xb.at[slot, mine], xb.at[slot, mine], x_sem.at[slot + 1], sibling)
    for slot in (2, 3):
        arrived(xb.at[slot, other], x_sem.at[slot + 1])
        norm_rows(xb.at[slot], nb, 128 * slot, 128, shift, scale1)
    project(nb[256:512, :], wvb, qkv_ref, 256, gains_ref[0:1, :], gains_ref[1:2, :])
    arrived(wsv_ref, w_sem.at[0])
    arrived(wst_ref, w_sem.at[1])
    sends.finish()


def attend(qb, q0, count, keys, values, acc, first, mask=None):
    for h in range(NH):
        lanes = slice(h * HD, (h + 1) * HD)
        query = qb[pl.ds(q0, count), lanes]
        total = None
        for key_ref, value_ref in zip(keys, values):
            scores = lax.dot_general(
                query, key_ref[:, lanes], (((1,), (1,)), ((), ())), preferred_element_type=F32)
            expo = jnp.exp2(scores * EXP_SCALE)
            if mask is not None:
                expo = jnp.where(mask, expo, 0.0)
            value = value_ref[:, lanes]
            wide = jnp.concatenate([value, jnp.ones_like(value)], axis=1)
            part = jnp.dot(expo.astype(BF16), wide, preferred_element_type=F32)
            total = part if total is None else total + part
        if first:
            acc[h, pl.ds(q0, count), :] = total
        else:
            acc[h, pl.ds(q0, count), :] += total


def coded_denoms(acc, rows):
    parts = [acc[h, rows, HD:] for h in range(NH)]
    lane = lax.broadcasted_iota(jnp.int32, parts[0].shape, 1)
    return jnp.where(lane < 8, parts[0], jnp.where(lane < 16, parts[1], parts[2]))


def attention_kernel(qkv_ref, tqkv_ref, len_ref, attn_ref, text_ref,
                     qb, kvb, tkv, acc, osend, dsend, orecv, drecv, tsend, trecv, afin, tfin,
                     send_sem, kv_sem, q_sem, t_sem, o_sem, tr_sem, out_sem):
    x, y, z, c = coords()
    zh = z // 2
    zl = lax.rem(z, 2)
    role = lax.rem(c + zh, 2)
    is0, is1 = role == 0, role == 1
    sibling = dev(x, y, z, 1 - c)
    xp, xm = dev(x + 1, y, z, c), dev(x - 1, y, z, c)
    yps = {1: dev(x, y + 1, z, c), 2: dev(x, y - 1, z, c), 3: dev(x, y + 2, z, c)}
    owner = role == y // 2
    owner_self = jnp.logical_and(owner, lax.rem(x, 2) == c)

    barrier = pltpu.get_barrier_semaphore()
    for device in (sibling, xp, xm, yps[1], yps[2], yps[3], dev(x, y, z + 2, zh)):
        signal(barrier, device)

    @pl.when(is1)
    def _():
        signal(barrier, dev(x, y, z + 2, 1 - zh))

    for xi in range(2):
        for sy in range(4):
            for sz in range(2):
                source_core = (sz + sy // 2) % 2
                sx = c + 2 * xi
                same = jnp.logical_and(
                    jnp.logical_and(sx == x, sy == y), jnp.logical_and(sz == zh, source_core == c))

                @pl.when(jnp.logical_not(same))
                def _():
                    signal(barrier, (sx, sy, sz, zl, source_core))

    pl.semaphore_wait(
        barrier, 7 + role + jnp.where(owner, 32, 0) - jnp.where(owner_self, 1, 0))

    sends = Sends(send_sem, sibling)

    def arrived(dst, sem):
        pltpu.make_async_remote_copy(
            src_ref=dst, dst_ref=dst, send_sem=send_sem.at[0], recv_sem=sem,
            device_id=sibling, device_id_type=MESH).wait_recv()

    q_own = qb.at[pl.ds(0, BLK)]
    tq_own = qb.at[pl.ds(BLK, TQ)]

    def q_slot(pos):
        return qb.at[pl.ds(OWN + (pos - 1) * BLK, BLK)]

    tq_row = pl.multiple_of(64 * x, 64)
    tq_other = tqkv_ref.at[0, pl.ds(pl.multiple_of(64 * x + TQ, TQ), TQ)]
    tkv_src = tqkv_ref.at[pl.ds(1, 2)]
    kv_src = qkv_ref.at[pl.ds(1, 2)]
    q_src = qkv_ref.at[0]
    partner = dev(x, y, z + 2, 1 - c)
    local = [
        (q_src, q_own, q_sem.at[0]),
        (kv_src, kvb.at[0, 0], kv_sem.at[0, 0, 0]),
        (tqkv_ref.at[0, pl.ds(tq_row, TQ)], tq_own, t_sem.at[0]),
        (tkv_src, tkv, t_sem.at[1]),
    ]

    def send_queries(pred):
        for pos, back in ((1, 2), (2, 1), (3, 3)):
            sends.start(q_own, q_slot(back), q_sem.at[back], yps[pos], pred)

    def send_own(r, pred):
        def block():
            return kvb.at[r, 0]

        sends.start(block, kvb.at[r, 2], kv_sem.at[r, 2, 0], xp, pred)
        sends.start(block, kvb.at[r, 1], kv_sem.at[r, 1, 0], xm, pred)
        sends.start(block, block(), kv_sem.at[r, 0, 0], sibling, pred)

    def pass_on(r, pred):
        arrived(kvb.at[r, 1], kv_sem.at[r, 1, 0])
        sends.start(lambda: kvb.at[r, 1, 0], kvb.at[r, 3, 0], kv_sem.at[r, 3, 0], xm, pred)
        arrived(kvb.at[r, 2], kv_sem.at[r, 2, 0])
        sends.start(lambda: kvb.at[r, 2, 1], kvb.at[r, 3, 1], kv_sem.at[r, 3, 1], xp, pred)
        for pos in (1, 2):
            sends.start(lambda pos=pos: kvb.at[r, pos], kvb.at[r, pos], kv_sem.at[r, pos, 0], sibling, pred)

    def pass_last(r, pred):
        for part in range(2):
            arrived(kvb.at[r, 3, part], kv_sem.at[r, 3, part])
        sends.start(lambda: kvb.at[r, 3], kvb.at[r, 3], kv_sem.at[r, 3, 0], sibling, pred)

    @pl.when(is0)
    def _():
        for src, dst, sem in local:
            pltpu.make_async_copy(src, dst, sem).start()
        sends.start(tq_other, tq_own, t_sem.at[0], sibling, is0)
        sends.start(tkv_src, tkv, t_sem.at[1], sibling, is0)
        for src, dst, sem in local:
            pltpu.make_async_copy(src, dst, sem).wait()
        send_own(0, is0)
        send_queries(is0)

    @pl.when(is1)
    def _():
        sends.start(q_src, q_own, q_sem.at[0], partner, is1)
        sends.start(kv_src, kvb.at[1, 0], kv_sem.at[1, 0, 0], partner, is1)
        arrived(q_own, q_sem.at[0])
        send_queries(is1)
        arrived(tq_own, t_sem.at[0])
        arrived(tkv, t_sem.at[1])

    shape = (OWN, TXT)
    row = lax.broadcasted_iota(jnp.int32, shape, 0)
    col = lax.broadcasted_iota(jnp.int32, shape, 1)
    row_limit = jnp.where(y == 0, OWN, BLK)
    mask = jnp.logical_and(col < len_ref[0], row < row_limit)
    attend(qb, 0, OWN, [tkv.at[0]], [tkv.at[1]], acc, True, mask)

    @pl.when(is1)
    def _():
        arrived(kvb.at[0, 0], kv_sem.at[0, 0, 0])

    attend(qb, 0, OWN, [kvb.at[0, 0, 0]], [kvb.at[0, 0, 1]], acc, False)

    @pl.when(is1)
    def _():
        arrived(kvb.at[1, 0], kv_sem.at[1, 0, 0])
        send_own(1, is1)

    arrived(q_slot(1), q_sem.at[1])
    arrived(q_slot(2), q_sem.at[2])
    attend(qb, OWN, 2 * BLK, [kvb.at[0, 0, 0]], [kvb.at[0, 0, 1]], acc, True)

    @pl.when(is0)
    def _():
        pass_on(0, is0)

    arrived(q_slot(3), q_sem.at[3])
    attend(qb, OWN + 2 * BLK, BLK, [kvb.at[0, 0, 0]], [kvb.at[0, 0, 1]], acc, True)

    def middle(n, carry):
        block = 1 + n // 2
        r, pos = block // 4, lax.rem(block, 4)
        half = lax.rem(n, 2)

        for when, want in ((0, 1), (2, 2), (4, 3)):
            @pl.when(jnp.logical_and(n == when, is1))
            def _(want=want):
                arrived(kvb.at[0, want], kv_sem.at[0, want, 0])

        @pl.when(jnp.logical_and(n == 2, is0))
        def _():
            pass_last(0, is0)

        @pl.when(jnp.logical_and(n == 2, is1))
        def _():
            pass_on(1, is1)

        @pl.when(jnp.logical_and(n == 6, is1))
        def _():
            pass_last(1, is1)

        @pl.when(jnp.logical_and(n == 6, is0))
        def _():
            arrived(kvb.at[1, 0], kv_sem.at[1, 0, 0])

        q0 = pl.multiple_of(half * (QROWS // 2), 16)
        attend(qb, q0, QROWS // 2, [kvb.at[r, pos, 0]], [kvb.at[r, pos, 1]], acc, False)
        return carry

    lax.fori_loop(0, 8, middle, 0)

    @pl.when(is0)
    def _():
        for pos in (1, 2, 3):
            arrived(kvb.at[1, pos], kv_sem.at[1, pos, 0])

    last_keys = [kvb.at[1, pos, 0] for pos in (1, 2, 3)]
    last_values = [kvb.at[1, pos, 1] for pos in (1, 2, 3)]
    for pos, back in ((3, 3), (1, 2), (2, 1)):
        q0 = OWN + (pos - 1) * BLK
        rows = pl.ds(q0, BLK)
        attend(qb, q0, BLK, last_keys, last_values, acc, False)
        for h in range(NH):
            osend[pos - 1, :, h * HD : (h + 1) * HD] = acc[h, rows, :HD].astype(BF16)
        dsend[pos - 1] = jnp.transpose(coded_denoms(acc, rows))[:24]
        sends.start(osend.at[pos - 1], orecv.at[back - 1], o_sem.at[back - 1, 0], yps[pos])
        sends.start(dsend.at[pos - 1], drecv.at[back - 1], o_sem.at[back - 1, 1], yps[pos])
    attend(qb, 0, OWN, last_keys, last_values, acc, False)

    for p in range(2):
        rows = pl.ds(BLK + 16 * p, 16)
        target = 2 * role + p
        for h in range(NH):
            tsend[p, :, h * HD : (h + 1) * HD] = acc[h, rows, :HD]
        tsend[p, :, W:] = coded_denoms(acc, rows)

        elsewhere = target != y

        @pl.when(elsewhere)
        def _():
            sends.start(lambda p=p: tsend.at[p], trecv.at[y], tr_sem.at[y], dev(x, target, z, c), elsewhere)

    core = lax.rem(x, 2)
    to_sibling = jnp.logical_and(owner, core != c)

    @pl.when(owner)
    def _():
        for sy in range(4):
            @pl.when(sy != y)
            def _():
                arrived(trecv.at[sy], tr_sem.at[sy])

        total = tsend[y - 2 * role]
        for sy in range(4):
            total = total + jnp.where(sy != y, trecv[sy], 0.0)
        for h in range(NH):
            denom = total[:, W + 8 * h : W + 8 * h + 1]
            tfin[:, h * HD : (h + 1) * HD] = (total[:, h * HD : (h + 1) * HD] / denom).astype(BF16)
        trow = pl.multiple_of(lax.rem(x // 2, 2) * 64 + 16 * y, 16)
        tcol = pl.multiple_of(zh * W, HD)
        place = text_ref.at[pl.ds(trow, 16), pl.ds(tcol, W)]
        for dx in range(4):
            for dy in range(4):
                for dz in range(2):
                    if dx + dy + dz == 0:
                        continue
                    sends.start(tfin, place, out_sem.at[1], dev(x + dx, y + dy, z + 2 * dz, core), owner)

        @pl.when(core == c)
        def _():
            pltpu.make_async_copy(tfin, place, out_sem.at[1]).start()

        @pl.when(core != c)
        def _():
            sends.start(tfin, place, out_sem.at[1], sibling, to_sibling)

    for pos in (3, 1, 2):
        arrived(orecv.at[pos - 1], o_sem.at[pos - 1, 0])
        arrived(drecv.at[pos - 1], o_sem.at[pos - 1, 1])
    denoms = drecv[0] + drecv[1] + drecv[2]
    for h in range(NH):
        lanes = slice(h * HD, (h + 1) * HD)
        numer = acc[h, 0:BLK, :HD]
        for pos in range(3):
            numer = numer + orecv[pos, :, lanes].astype(F32)
        denom = acc[h, 0:BLK, HD:] + jnp.transpose(
            jnp.broadcast_to(denoms[8 * h : 8 * h + 1, :], (HD, BLK)))
        afin[:, lanes] = (numer / denom).astype(BF16)

    acol = pl.ds(pl.multiple_of(zh * W, HD), W)
    for core in range(2):
        for slot in range(2):
            src = afin.at[pl.ds((2 * slot + core) * 128, 128)]
            dst = attn_ref.at[slot, :, acol]
            across = jnp.logical_and(is0, c != core)

            @pl.when(is1)
            def _():
                sends.start(src, dst, out_sem.at[0], dev(x, y, z + 2, core), is1)

            @pl.when(jnp.logical_and(is0, c == core))
            def _():
                pltpu.make_async_copy(src, dst, out_sem.at[0]).start()

            @pl.when(across)
            def _():
                sends.start(src, dst, out_sem.at[0], sibling, across)

    arrived(text_ref, out_sem.at[1])
    arrived(attn_ref, out_sem.at[0])
    sends.finish()


CH = 768
NCH = D // CH


def output_kernel(attn_ref, text_ref, wv_ref, wsv_ref, wt_ref, wst_ref, mod_ref, len_ref, step_ref,
                  video_out_ref, text_out_ref,
                  wvb, wtb, modb, fsend, frecv, tsend, trecv, load_sem, send_sem, recv_sem):
    x, y, z, c = coords()
    zl = lax.rem(z, 2)
    ours = pl.ds(pl.multiple_of(c * W, 16), W)
    theirs = pl.ds(pl.multiple_of((1 - c) * W, 16), W)
    loads = [
        pltpu.make_async_copy(wv_ref, wvb.at[ours], load_sem.at[0]),
        pltpu.make_async_copy(wsv_ref, wvb.at[theirs], load_sem.at[1]),
        pltpu.make_async_copy(wt_ref, wtb.at[ours], load_sem.at[2]),
        pltpu.make_async_copy(wst_ref, wtb.at[theirs], load_sem.at[3]),
        pltpu.make_async_copy(mod_ref.at[2], modb.at[0], load_sem.at[4]),
        pltpu.make_async_copy(mod_ref.at[5], modb.at[1], load_sem.at[5]),
    ]
    for copy in loads:
        copy.start()
    toward = 1 - 2 * c
    target = dev(x, y, z + toward, c)
    barrier = pltpu.get_barrier_semaphore()
    signal(barrier, dev(x, y, z - toward, c))
    pl.semaphore_wait(barrier, 1)
    sends = Sends(send_sem, target)
    loads[0].wait()
    loads[1].wait()
    for i in range(NCH):
        cols = slice(i * CH, (i + 1) * CH)
        fsend[i] = jnp.dot(attn_ref[1], wvb[:, cols], preferred_element_type=F32).astype(BF16)
        sends.start(fsend.at[i], frecv.at[i], recv_sem.at[0, i], target)
    loads[2].wait()
    loads[3].wait()
    own_row = pl.multiple_of(zl * 64, 64)
    far_row = pl.multiple_of((1 - zl) * 64, 64)
    for i in range(NCH):
        cols = slice(i * CH, (i + 1) * CH)
        tsend[i] = jnp.dot(
            text_ref[pl.ds(far_row, 64), :], wtb[:, cols], preferred_element_type=F32).astype(BF16)
        sends.start(tsend.at[i], trecv.at[i], recv_sem.at[1, i], target)
    loads[4].wait()
    loads[5].wait()
    step = step_ref[0]

    def arrived(dst, sem):
        pltpu.make_async_remote_copy(
            src_ref=dst, dst_ref=dst, send_sem=send_sem.at[0], recv_sem=sem,
            device_id=target, device_id_type=MESH).wait_recv()

    for i in range(NCH):
        cols = slice(i * CH, (i + 1) * CH)
        own = jnp.dot(attn_ref[0], wvb[:, cols], preferred_element_type=F32)
        arrived(frecv.at[i], recv_sem.at[0, i])
        gate = modb[0, pl.ds(step, 1), cols]
        video_out_ref[:, cols] = (gate * (own + frecv[i].astype(F32))).astype(BF16)
    row = lax.broadcasted_iota(jnp.int32, (64, CH), 0) + (zl * 2 + c) * 64
    valid = row < len_ref[0]
    for i in range(NCH):
        cols = slice(i * CH, (i + 1) * CH)
        own = jnp.dot(text_ref[pl.ds(own_row, 64), :], wtb[:, cols], preferred_element_type=F32)
        arrived(trecv.at[i], recv_sem.at[1, i])
        gate = modb[1, pl.ds(step, 1), cols]
        text_out_ref[:, cols] = jnp.where(
            valid, gate * (own + trecv[i].astype(F32)), 0.0).astype(BF16)
    sends.finish()


ANY = pl.BlockSpec(memory_space=pl.ANY)
VMEM = pl.BlockSpec(memory_space=pltpu.VMEM)
SMEM = pl.BlockSpec(memory_space=pltpu.SMEM)
DMA = pltpu.SemaphoreType.DMA


def params(ident):
    return pltpu.CompilerParams(
        collective_id=ident, has_side_effects=True, vmem_limit_bytes=VMEM_LIMIT)


def body(x_video, x_text, w_qkv_video, w_qkv_text, w_out_video, w_out_text, qk_gains, modulation,
         text_len, timestep):
    wv = jnp.transpose(w_qkv_video, (1, 0, 2))
    wt = jnp.transpose(w_qkv_text, (1, 0, 2))
    mod = jnp.transpose(modulation, (1, 0, 2))
    shape = jax.ShapeDtypeStruct
    steps = modulation.shape[0]
    qkv, tqkv, wsv, wst = pl.pallas_call(
        qkv_kernel,
        name="qkv",
        in_specs=[ANY, ANY, ANY, ANY, ANY, VMEM, ANY, ANY, SMEM],
        out_specs=[VMEM, VMEM, ANY, ANY],
        out_shape=[shape((3, BLK, W), BF16), shape((3, TXT, W), BF16),
                   shape((W, D), BF16), shape((W, D), BF16)],
        scratch_shapes=[
            pltpu.VMEM((4, 128, D), BF16), pltpu.VMEM((TXT, D), BF16),
            pltpu.VMEM((D, 3 * W), BF16), pltpu.VMEM((D, 3 * W), BF16),
            pltpu.VMEM((6, steps, D), F32), pltpu.VMEM((BLK, D), BF16),
            DMA((9,)), DMA((8,)), DMA((5,)), DMA((2,))],
        compiler_params=params(1),
    )(x_video, x_text, wv, wt, mod, qk_gains, w_out_video, w_out_text, timestep)
    attn, text = pl.pallas_call(
        attention_kernel,
        name="attention",
        in_specs=[ANY, ANY, SMEM],
        out_specs=[ANY, ANY],
        out_shape=[shape((2, 128, 2 * W), BF16), shape((128, 2 * W), BF16)],
        scratch_shapes=[
            pltpu.VMEM((QROWS, W), BF16), pltpu.VMEM((2, 4, 2, BLK, W), BF16),
            pltpu.VMEM((2, TXT, W), BF16), pltpu.VMEM((NH, QROWS, 2 * HD), F32),
            pltpu.VMEM((3, BLK, W), BF16), pltpu.VMEM((3, 24, BLK), F32),
            pltpu.VMEM((3, BLK, W), BF16), pltpu.VMEM((3, 24, BLK), F32),
            pltpu.VMEM((2, 16, W + HD), F32), pltpu.VMEM((4, 16, W + HD), F32),
            pltpu.VMEM((BLK, W), BF16), pltpu.VMEM((16, W), BF16),
            DMA((80,)), DMA((2, 4, 2)), DMA((4,)), DMA((2,)), DMA((3, 2)), DMA((4,)), DMA((2,))],
        compiler_params=params(2),
    )(qkv, tqkv, text_len)
    return tuple(pl.pallas_call(
        output_kernel,
        name="output",
        in_specs=[VMEM, VMEM, ANY, ANY, ANY, ANY, ANY, SMEM, SMEM],
        out_specs=[VMEM, VMEM],
        out_shape=[shape((128, D), BF16), shape((64, D), BF16)],
        scratch_shapes=[
            pltpu.VMEM((2 * W, D), BF16), pltpu.VMEM((2 * W, D), BF16),
            pltpu.VMEM((2, steps, D), F32),
            pltpu.VMEM((NCH, 128, CH), BF16), pltpu.VMEM((NCH, 128, CH), BF16),
            pltpu.VMEM((NCH, 64, CH), BF16), pltpu.VMEM((NCH, 64, CH), BF16),
            DMA((6,)), DMA((2 * NCH,)), DMA((2, NCH))],
        compiler_params=params(3),
    )(attn, text, w_out_video, wsv, w_out_text, wst, mod, text_len, timestep))


def solution(mesh):
    grid = Mesh(mesh.devices.reshape(4, 4, 2, 2, 2), AXES)
    head = ("zl", "c")
    return jax.shard_map(
        body,
        mesh=grid,
        in_specs=(P(AXES, None), P(), P(None, None, head), P(None, None, head),
                  P(head, None), P(head, None), P(), P(), P(), P()),
        out_specs=(P(AXES, None), P(head, None)),
        check_vma=False,
    )
```

time: 1070 us -> 130 us (0.12)
  waiting for transfers between devices: 562 us -> 0 us
  matrix products: 224 us -> 0 us
  local copies, waits for them, and re-layouts: 145 us -> 3.83 us
  Pallas kernels: 0 us -> 124 us
  blocking collectives: 85.1 us -> 0 us
  other arithmetic: 30.3 us -> 0 us
  between operations: 15.8 us -> 1.95 us
    all_gather x3 -> x0, waiting for transfers between devices: 274 us -> none  [the longest x1 143 us: body(): lax.all_gather(k_video, 'blk', axis=0, tiled=True)]
    psum x1 -> x0, waiting for transfers between devices: 228 us -> none  [body(): summed_numer, summed_denom = lax.psum((local_numer, local_denom), 'blk')]
    dot_general x74 -> x0, matrix products: 224 us -> none  [the longest x35 113 us: partial_scores(): jnp.einsum('qhd,khd->hqk', query_split, key_split, preferred_element_type...]
    pallas_call x0 -> x3, Pallas kernels: none -> 124 us  [the longest x1 80.6 us: body(): pl.pallas_call(attention_kernel, name='attention', in_specs=[ANY, ANY, SM...]
    psum x1 -> x0, blocking collectives: 85.1 us -> none  [body(): summed_numer, summed_denom = lax.psum((local_numer, local_denom), 'blk')]
    reduce_scatter x2 -> x0, waiting for transfers between devices: 58.6 us -> none  [the longest x1 58.6 us: body(): lax.psum_scatter(jnp.dot(block, w_out_video, preferred_element_type=jnp.f...]
    while x256 -> x0, local copies, waits for them, and re-layouts: 52.1 us -> none
    dynamic_slice x96 -> x0, local copies, waits for them, and re-layouts: 50.3 us -> none  [add_keys(): result, unused = lax.scan(advance, running, (key_blocks, value_blocks))]
  transfers between devices with their start and end apart: 6 -> 0, of which waited for: 4 -> 0; matrix products, arithmetic and copies ran while one was open for 30% -> 0% of each run, Pallas kernels for 0% -> 0%
where the time goes in v1:
time: 130 us
  Pallas kernels  124 us (95%)
  local copies, waits for them, and re-layouts  3.83 us (3%)
  between operations  1.95 us (2%)
    pallas_call x1, Pallas kernels, body(): pl.pallas_call(attention_kernel, name='attention', in_specs=[ANY, ANY, SM...  80.6 us
    pallas_call x1, Pallas kernels, body(): pl.pallas_call(qkv_kernel, name='qkv', in_specs=[ANY, ANY, ANY, ANY, ANY,...  23.1 us
    pallas_call x1, Pallas kernels, body(): pl.pallas_call(output_kernel, name='output', in_specs=[VMEM, VMEM, ANY, A...  20.1 us
    unnamed x2, local copies, waits for them, and re-layouts  3.83 us

profile of v1, /device:TPU:1, one launch (start us, length us, event | category | flops | bytes accessed | tf_op | source)
XLA Modules:
  0.0 129.6 jit_solution(17201344817561597277)
XLA Ops:
  1.9 23.1 %qkv.1 = (bf16[3,512,384]{2,1,0:T(8,128)(2,1)}, bf16[3,256,384]{2,1,0:T(8,128)(2,1)}, bf16[384,3072]{1,0:T(8,128)(2,1)}, bf16[384,3072]{1,0:T(8,128)(2,1)}) custom-call(bf16[128,3072]{1,0:T(8,128)(2,1)} %x_ref.1, bf16[256,3072]{1,0:T(8,128)(2,1)} %xt_ref.1, bf16[3,3072,384]{2,1,0:T(8,128)(2,1)} %bitcast.5, bf16[3,3072,384]{2,1,0:T(8,128)(2,1)} %bitcast.6, ...), custom_call_target="tpu_custom_call" | custom-call | tf_op jit(solution)/shard_map/qkv/pallas_call | solution.py:554
  25.0 80.6 %attention.1 = (bf16[2,128,768]{2,1,0:T(8,128)(2,1)}, bf16[128,768]{1,0:T(8,128)(2,1)}) custom-call(bf16[3,512,384]{2,1,0:T(8,128)(2,1)} %get-tuple-element.8.qkv_ref, bf16[3,256,384]{2,1,0:T(8,128)(2,1)} %get-tuple-element.9.tqkv_ref, s32[1]{0:T(128)S(6)} %copy.14.len_ref), custom_call_target="tpu_custom_call" | custom-call | tf_op jit(solution)/shard_map/attention/pallas_call | solution.py:568
  105.6 20.1 %output.1 = (bf16[128,3072]{1,0:T(8,128)(2,1)}, bf16[64,3072]{1,0:T(8,128)(2,1)}) custom-call(bf16[2,128,768]{2,1,0:T(8,128)(2,1)} %get-tuple-element.10.attn_ref, bf16[128,768]{1,0:T(8,128)(2,1)} %get-tuple-element.11.text_ref, bf16[384,3072]{1,0:T(8,128)(2,1)} %wv_ref.1, bf16[384,3072]{1,0:T(8,128)(2,1)} %get-tuple-element.12.wsv_ref, ...), custom_call_target="tpu_custom_call" | custom-call | tf_op jit(solution)/shard_map/output/pallas_call | solution.py:584
  125.7 2.1 %copy.16 = bf16[128,3072]{1,0:T(8,128)(2,1)} copy(bf16[128,3072]{1,0:T(8,128)(2,1)} %get-tuple-element.16) | data formatting | bytes 1572864
  127.8 1.8 %copy.17 = bf16[64,3072]{1,0:T(8,128)(2,1)} copy(bf16[64,3072]{1,0:T(8,128)(2,1)} %get-tuple-element.17) | data formatting | bytes 786432
